TPU v7x, 768 devices: a whole 4x8x12 slice. The times are simulated.
768 devices in a mesh: dp: 12 (over z_lo, core), node: 64 (over z_hi, y, x).
Axes of the slice: x: 4, y: 8, z: 12 (z_hi: 2, z_lo: 6; z = z_hi * 6 + z_lo), core: 2. Of those that a mesh axis runs over, the one named last changes fastest.
Arguments:
- tokens: bfloat16 [196608, 2048], P(('dp', 'node')), may hold values from -6 to 6
- key_cot: bfloat16 [196608, 256], P(('dp', 'node')), may hold values from -6 to 6
- value_cot: bfloat16 [196608, 256], P(('dp', 'node')), may hold values from -6 to 6
- key_mant: bfloat16 [2048, 256], P('node'), may hold values from -0.125 to 0.125
- value_mant: bfloat16 [2048, 256], P('node'), may hold values from -0.125 to 0.125
- key_expo: int32 [2048, 2], P('node'), may hold values from -2 to 1
- value_expo: int32 [2048, 2], P('node'), may hold values from -2 to 1
Outputs:
- keys: bfloat16 [196608, 256], P(('dp', 'node'))
- values: bfloat16 [196608, 256], P(('dp', 'node'))
- tokens_grad: bfloat16 [196608, 2048], P(('dp', 'node'))
- key_grad: float32 [2048, 256], P('node')
- value_grad: float32 [2048, 256], P('node')
All inputs are finite; a program needn't handle non-finite values.
Results may differ from a plain program's by a relative error of at most 0.001.
Values may be sent and summed in bfloat16 or wider, within the bound.
A program may use at most 32 MiB of HBM per device.

v0:
```python
import math

import jax
import jax.numpy as jnp
from jax import lax
from jax.sharding import PartitionSpec as P

BLOCK = 128


def dequant(mant, expo):
    factor = jnp.zeros(expo.shape, jnp.float32)
    for exponent in range(-2, 2):
        factor = factor + jnp.where(expo == exponent, jnp.float32(2.0**exponent), jnp.float32(0.0))
    blocks = mant.astype(jnp.float32).reshape(mant.shape[0], expo.shape[1], BLOCK)
    return (blocks * factor[:, :, None]).reshape(mant.shape).astype(jnp.bfloat16)


def over_rows(left, right):
    return lax.dot_general(
        left, right, (((0,), (0,)), ((), ())), preferred_element_type=jnp.float32
    )


def over_cols(left, right):
    return lax.dot_general(
        left, right, (((1,), (1,)), ((), ())), preferred_element_type=jnp.float32
    )


def on_device(tokens, key_cot, value_cot, key_mant, value_mant, key_expo, value_expo):
    all_kmant, all_vmant, all_kexpo, all_vexpo = (
        lax.all_gather(key_mant, "node", axis=0, tiled=True),
        lax.all_gather(value_mant, "node", axis=0, tiled=True),
        lax.all_gather(key_expo, "node", axis=0, tiled=True),
        lax.all_gather(value_expo, "node", axis=0, tiled=True),
    )
    key_w = dequant(all_kmant, all_kexpo)
    value_w = dequant(all_vmant, all_vexpo)
    keys = jnp.dot(tokens, key_w, preferred_element_type=jnp.float32).astype(jnp.bfloat16)
    values = jnp.dot(tokens, value_w, preferred_element_type=jnp.float32).astype(jnp.bfloat16)
    back_key, back_value = (
        lax.all_gather(dequant(key_mant, key_expo), "node", axis=0, tiled=True),
        lax.all_gather(dequant(value_mant, value_expo), "node", axis=0, tiled=True),
    )
    tokens_grad = (over_cols(key_cot, back_key) + over_cols(value_cot, back_value)).astype(
        jnp.bfloat16
    )
    key_term = over_rows(tokens, key_cot)
    value_term = over_rows(tokens, value_cot)
    key_part, value_part = (
        lax.psum_scatter(key_term, "node", scatter_dimension=0, tiled=True),
        lax.psum_scatter(value_term, "node", scatter_dimension=0, tiled=True),
    )
    key_sum, value_sum = lax.psum((key_part, value_part), "dp")
    total_rows = tokens.shape[0] * lax.axis_size("dp") * lax.axis_size("node")
    scale = jnp.float32(1.0 / math.sqrt(total_rows))
    return (keys, values, tokens_grad, key_sum * scale, value_sum * scale)


def solution(mesh):
    in_specs = (
        P(("dp", "node"), None),
        P(("dp", "node"), None),
        P(("dp", "node"), None),
        P("node", None),
        P("node", None),
        P("node", None),
        P("node", None),
    )
    out_specs = (
        P(("dp", "node"), None),
        P(("dp", "node"), None),
        P(("dp", "node"), None),
        P("node", None),
        P("node", None),
    )
    return jax.shard_map(
        on_device, mesh=mesh, in_specs=in_specs, out_specs=out_specs, check_vma=False
    )
```

profile of v0, /device:TPU:1, one launch (start us, length us, event | category | flops | bytes accessed | tf_op | source)
XLA Modules:
  0.0 1757.1 jit_solution(6877872580435564170)
XLA Ops:
  7.2 0.0 all-gather.11.cloned.1.call-start
  7.2 0.8 fusion.16
  8.0 0.1 copy.34
  8.1 0.1 mul.56
  8.2 1.3 fusion.13
  9.5 0.0 all-gather.11.cloned.1.call-update
  9.5 0.0 all-gather.7.cloned.1.call-start
  9.6 0.7 all-gather.7.cloned.1.call-update
  10.3 0.0 all-gather.9.cloned.1.call-start
  10.3 0.7 all-gather.9.cloned.1.call-update
  11.0 0.0 reduce-scatter.3.cloned.1.call-start
  11.1 2.7 fusion.21
  13.8 0.0 reduce-scatter.3.cloned.1.call-update
  13.9 0.0 reduce-scatter.5.cloned.1.call-start
  13.9 1.8 fusion.22
  15.7 0.0 reduce-scatter.5.cloned.1.call-update
  15.8 0.0 all-gather.13.cloned.1.call-start
  15.8 0.1 copy.35
  15.9 0.1 mul.59
  16.0 0.6 fusion.12
  16.6 0.0 all-gather.13.cloned.1.call-update
  16.7 0.0 all-reduce.3.cloned.1.call-start
  16.7 243.4 %all-gather = s32[64,32,2]{1,2,0:T(2,128)S(1)} all-gather(s32[1,32,2]{1,2,0:T(2,128)S(1)} %bitcast.52), channel_id=1, replica_groups=mesh['dp'=12,'node'=64] {'node'}, dimensions={0}, use_global_device_ids=true | all-gather | bytes 16640 | tf_op jit(solution)/shard_map/all_gather | solution.py:35
  260.2 0.1 compare_select_fusion.4
  260.3 0.1 reshape.72
  260.4 0.1 reshape.57
  260.5 1.3 copy.30
  261.9 227.6 %all-gather.1 = s32[64,32,2]{1,2,0:T(2,128)S(1)} all-gather(s32[1,32,2]{1,2,0:T(2,128)S(1)} %bitcast.53), channel_id=1, replica_groups=mesh['dp'=12,'node'=64] {'node'}, dimensions={0}, use_global_device_ids=true | all-gather | bytes 16640 | tf_op jit(solution)/shard_map/all_gather | solution.py:36
  489.5 0.1 compare_select_fusion
  489.6 0.1 reshape.73
  489.7 0.1 reshape.69
  489.8 1.5 copy.33
  491.3 1.7 fusion.20
  493.0 0.0 all-gather.7.cloned.1.call-done
  493.0 5.1 mul.50
  498.1 0.7 fusion.4
  498.8 0.0 all-gather.9.cloned.1.call-done
  498.9 5.1 mul.53
  504.0 0.7 fusion.5
  504.7 415.3 %reduce-scatter.3.cloned.1.call-done = f32[32,256]{1,0:T(8,128)} async-done(((f32[2048,256]{1,0:T(8,128)}), f32[32,256]{1,0:T(8,128)}) %reduce-scatter.3.cloned.1.call-update) | async-done | bytes 32784 | tf_op jit(solution)/shard_map/reduce_scatter | solution.py:52
  920.0 517.1 %reduce-scatter.5.cloned.1.call-done = f32[32,256]{1,0:T(8,128)} async-done(((f32[2048,256]{1,0:T(8,128)}), f32[32,256]{1,0:T(8,128)}) %reduce-scatter.5.cloned.1.call-update) | async-done | bytes 32784 | tf_op jit(solution)/shard_map/reduce_scatter | solution.py:53
  1437.1 185.5 %all-gather.13.cloned.1.call-done = bf16[2048,256]{1,0:T(8,128)(2,1)} async-done(((bf16[32,256]{1,0:T(8,128)(2,1)}), bf16[2048,256]{1,0:T(8,128)(2,1)}) %all-gather.13.cloned.1.call-update) | async-done | bytes 1048592 | tf_op jit(solution)/shard_map/all_gather | solution.py:44
  1622.6 2.7 fusion.1
  1625.3 0.8 copy.36
  1626.1 0.8 copy.37
  1626.8 2.3 copy.38
  1629.1 119.8 %all-reduce.3.cloned.1.call-done = (f32[32,256]{1,0:T(8,128)}, f32[32,256]{1,0:T(8,128)}) async-done(((f32[32,256]{1,0:T(8,128)}, f32[32,256]{1,0:T(8,128)}), (f32[32,256]{1,0:T(8,128)}, f32[32,256]{1,0:T(8,128)})) %all-reduce.3.cloned.1.call-update) | async-done | bytes 65552 | tf_op jit(solution)/shard_map/psum | solution.py:55
  1748.9 1.4 broadcast_multiply_fusion
  (25 shorter events, 0.1 us)
Async XLA Ops:
  7.2 3.9 copy-start
  7.2 484.1 %all-gather.11.cloned.1.call-start = ((), (), s32[]{:S(2)}) async-start(), calls=%async_computation.4 | async-start | bytes 1064960 | tf_op jit(solution)/shard_map/all_gather | solution.py:43
  9.5 483.5 %all-gather.7.cloned.1.call-start = ((), (), s32[]{:S(2)}) async-start(), calls=%async_computation.2 | async-start | bytes 1064960 | tf_op jit(solution)/shard_map/all_gather | solution.py:33
  10.3 488.6 %all-gather.9.cloned.1.call-start = ((), (), s32[]{:S(2)}) async-start(), calls=%async_computation.3 | async-start | bytes 1064960 | tf_op jit(solution)/shard_map/all_gather | solution.py:34
  11.0 2.9 copy-start.4
  11.0 908.9 %reduce-scatter.3.cloned.1.call-start = ((), (), s32[]{:S(2)}) async-start(), calls=%async_computation.6 | async-start | bytes 2129920 | tf_op jit(solution)/shard_map/reduce_scatter | solution.py:52
  13.8 2.0 copy-start.7
  13.9 2.2 copy-start.5
  13.9 2.9 copy-start.6
  13.9 1423.2 %reduce-scatter.5.cloned.1.call-start = ((), (), s32[]{:S(2)}) async-start(), calls=%async_computation.7 | async-start | bytes 2129920 | tf_op jit(solution)/shard_map/reduce_scatter | solution.py:53
  15.8 475.5 %copy-start.3 = (bf16[256,256]{1,0:T(8,128)(2,1)S(1)}, bf16[256,256]{1,0:T(8,128)(2,1)}, u32[]{:S(2)}) copy-start(bf16[256,256]{1,0:T(8,128)(2,1)} %param.8) | copy-start | bytes 393220
  15.8 1606.8 %all-gather.13.cloned.1.call-start = ((), (), s32[]{:S(2)}) async-start(), calls=%async_computation.5 | async-start | bytes 1064960 | tf_op jit(solution)/shard_map/all_gather | solution.py:44
  16.7 1732.2 %all-reduce.3.cloned.1.call-start = ((), (), s32[]{:S(2)}) async-start(), calls=%async_computation.8 | async-start | bytes 131072 | tf_op jit(solution)/shard_map/psum | solution.py:55
  493.0 5.1 copy-start.1
  498.8 5.1 copy-start.2
Sparse Core Ops, SparseCore 0:
  14.0 149.2 all-gather.10
  168.6 136.6 all-gather.6
  310.8 136.6 all-gather.8
  450.4 469.5 reduce-scatter.2
  923.2 513.8 reduce-scatter.4
  1442.9 179.6 all-gather.12
  1625.9 122.9 all-reduce.2
where the time goes:
time: 1760 us
  waiting for transfers between devices  1240 us (70%)
  blocking collectives  471 us (27%)
  local copies, waits for them, and re-layouts  17.6 us (1%)
    reduce_scatter x1, waiting for transfers between devices, on_device(): lax.psum_scatter(value_term, 'node', scatter_dimension=0, tiled=True)  517 us
    reduce_scatter x1, waiting for transfers between devices, on_device(): lax.psum_scatter(key_term, 'node', scatter_dimension=0, tiled=True)  415 us
    all_gather x1, blocking collectives, on_device(): lax.all_gather(key_expo, 'node', axis=0, tiled=True)  243 us
    all_gather x1, blocking collectives, on_device(): lax.all_gather(value_expo, 'node', axis=0, tiled=True)  228 us
    all_gather x1, waiting for transfers between devices, on_device(): lax.all_gather(dequant(value_mant, value_expo), 'node', axis=0, tiled=True)  186 us
    psum x1, waiting for transfers between devices, on_device(): key_sum, value_sum = lax.psum((key_part, value_part), 'dp')  120 us
  transfers between devices with their start and end apart: 7, of which 4 were waited for; matrix products, arithmetic and copies ran while one was open for 2% of the time, Pallas kernels for 0%

commit v1 on v0

v1 whole, which is shorter than its diff:
```python
import math

import jax
import jax.numpy as jnp
from jax import lax
from jax.experimental import pallas as pl
from jax.experimental.pallas import tpu as pltpu
from jax.sharding import PartitionSpec as P

MESH = pl.DeviceIdType.MESH
F32, BF16, I16 = jnp.float32, jnp.bfloat16, jnp.int16
NX, NY, NZ = 4, 8, 12
HALF = NZ // 2
ROWS = 32
COLS = 512
TOK = 256
DH = 1024
REDUCERS = 4
STEPS = 32766.0
TINY = 1e-30


def coordinates():
    dp, node = lax.axis_index("dp"), lax.axis_index("node")
    x = lax.rem(node, NX)
    y = lax.rem(node // NX, NY)
    half = node // (NX * NY)
    low = dp // 2
    core = lax.rem(dp, 2)
    return x, y, half, low, core


def device(x, y, z, core):
    return {
        "dp": lax.rem(z, HALF) * 2 + core,
        "node": (z // HALF) * (NX * NY) + y * NX + x,
    }


def shard_rows(mant, expo_t):
    factor = jnp.zeros(expo_t.shape, F32)
    for exponent in range(-2, 2):
        factor = factor + jnp.where(expo_t == exponent, F32(2.0**exponent), F32(0.0))
    parts = []
    for block in range(2):
        spread = lax.dot_general(
            factor[block : block + 1, :],
            jnp.ones((1, 128), F32),
            (((0,), (0,)), ((), ())),
            preferred_element_type=F32,
        )
        parts.append(mant[:, block * 128 : (block + 1) * 128].astype(F32) * spread)
    return jnp.concatenate(parts, axis=1).astype(BF16)


def over_rows(left, right):
    return lax.dot_general(left, right, (((0,), (0,)), ((), ())), preferred_element_type=F32)


def over_cols(left, right):
    return lax.dot_general(left, right, (((1,), (1,)), ((), ())), preferred_element_type=F32)


def kernel(
    tokens, key_cot, value_cot, key_mant, value_mant, key_expo, value_expo,
    keys, values, tokens_grad, key_grad, value_grad,
    tok, tok2, cot, cot2, mant, expo, part, codes, peaks, codes_in, peaks_in,
    sums, sums_in, total, total_in, final, own_w, other_w, tgrad, kv,
    load_sem, store_sem, send_c, recv_c, send_x, recv_x, send_y, recv_y,
    send_z, recv_z, send_g, recv_g, send_wz, recv_wz, send_wy, recv_wy, send_wx, recv_wx,
):
    x, y, half, low, core = coordinates()
    z = half * HALF + low
    sibling = device(x, y, z, 1 - core)
    home = core == half
    mine = pl.multiple_of(core * DH, DH)
    theirs = pl.multiple_of((1 - core) * DH, DH)

    def remote(src, dst, send, recv, to):
        return pltpu.make_async_remote_copy(
            src_ref=src, dst_ref=dst, send_sem=send, recv_sem=recv, device_id=to, device_id_type=MESH
        )

    loads = [
        pltpu.make_async_copy(key_mant, mant.at[0], load_sem.at[0]),
        pltpu.make_async_copy(value_mant, mant.at[1], load_sem.at[1]),
        pltpu.make_async_copy(key_expo, expo.at[0], load_sem.at[2]),
        pltpu.make_async_copy(value_expo, expo.at[1], load_sem.at[3]),
        pltpu.make_async_copy(tokens, tok, load_sem.at[4]),
        pltpu.make_async_copy(key_cot, cot.at[:, pl.ds(0, 256)], load_sem.at[5]),
        pltpu.make_async_copy(value_cot, cot.at[:, pl.ds(256, 256)], load_sem.at[6]),
    ]
    for load in loads:
        load.start()

    barrier = pltpu.get_barrier_semaphore()

    def greet(to):
        pl.semaphore_signal(barrier, inc=1, device_id=to, device_id_type=MESH)

    for d in range(1, NZ):
        greet(device(x, y, lax.rem(z + d, NZ), core))
    for d in range(1, NY):
        greet(device(x, lax.rem(y + d, NY), z, core))
    for d in range(1, NX):
        greet(device(lax.rem(x + d, NX), y, z, core))
    greet(sibling)

    for load in loads[:4]:
        load.wait()

    @pl.when(home)
    def _():
        own_w[y, x, :, 0:256] = shard_rows(mant[0], expo[0])
        own_w[y, x, :, 256:512] = shard_rows(mant[1], expo[1])

    for load in loads[4:]:
        load.wait()

    def own_part(j, _):
        left = tok[:, pl.ds(pl.multiple_of(mine + j * 128, 128), 128)]
        part[j] = over_rows(left, cot[...]).reshape(NX, ROWS, COLS)
        return 0

    lax.fori_loop(0, NY, own_part, 0)
    pl.semaphore_wait(barrier, (NZ - 1) + (NY - 1) + (NX - 1) + 1)

    swap_tok = remote(tok.at[:, pl.ds(theirs, DH)], tok2, send_c.at[0], recv_c.at[0], sibling)
    swap_cot = remote(cot, cot2, send_c.at[1], recv_c.at[1], sibling)
    swap_tok.start()
    swap_cot.start()

    across = device(x, y, lax.rem(z + HALF, NZ), core)
    w_z = remote(own_w.at[y, x], own_w.at[y, x], send_wz, recv_wz, across)

    @pl.when(home)
    def _():
        w_z.start()

    swap_tok.wait_recv()
    swap_cot.wait_recv()

    def encode(j, _):
        left = tok2[:, pl.ds(pl.multiple_of(j * 128, 128), 128)]
        part[j] = part[j] + over_rows(left, cot2[...]).reshape(NX, ROWS, COLS)
        for d in range(1, NX):
            chunk = part[j, lax.rem(x + d, NX)]
            peak = jnp.maximum(jnp.max(jnp.abs(chunk), axis=0, keepdims=True), TINY)
            codes[d - 1, j] = jnp.round(chunk * (STEPS / peak)).astype(jnp.int32).astype(I16)
            peaks[d - 1, j] = jnp.broadcast_to(peak * (1.0 / STEPS), (8, COLS))
        return 0

    def x_copies(part_of, d):
        to = device(lax.rem(x + d, NX), y, z, core)
        blocks = pl.ds(part_of * 4, 4)
        return (
            remote(codes.at[d - 1, blocks], codes_in.at[d - 1, blocks],
                   send_x.at[0, part_of, d - 1], recv_x.at[0, part_of, d - 1], to),
            remote(peaks.at[d - 1, blocks], peaks_in.at[d - 1, blocks],
                   send_x.at[1, part_of, d - 1], recv_x.at[1, part_of, d - 1], to),
        )

    for part_of in range(2):
        lax.fori_loop(part_of * 4, part_of * 4 + 4, encode, 0)
        for d in (2, 1, 3):
            for copy in x_copies(part_of, d):
                copy.start()

    @pl.when(jnp.logical_not(home))
    def _():
        w_z.wait_recv()

    def w_y(d, block):
        to = device(x, lax.rem(y + d, NY), z, core)
        return remote(own_w.at[block, x], own_w.at[block, x], send_wy.at[d - 1], recv_wy.at[d - 1], to)

    for d in (4, 3, 5, 2, 6, 1, 7):
        w_y(d, y).start()

    def add_x(j, _):
        value = part[j, x]
        for d in range(1, NX):
            scale = peaks_in[d - 1, j][0:1, :]
            value = value + codes_in[d - 1, j].astype(jnp.int32).astype(F32) * scale
        sums[j] = value
        return 0

    def y_copy(d, block):
        to = device(x, lax.rem(y + d, NY), z, core)
        return remote(sums.at[block], sums_in.at[d - 1], send_y.at[d - 1], recv_y.at[d - 1], to)

    for part_of in range(2):
        for d in (2, 1, 3):
            for copy in x_copies(part_of, d):
                copy.wait_recv()
        lax.fori_loop(part_of * 4, part_of * 4 + 4, add_x, 0)
        for d in (4, 3, 5, 2, 6, 1, 7):
            block = lax.rem(y + d, NY)

            @pl.when(block // 4 == part_of)
            def _(d=d, block=block):
                y_copy(d, block).start()

    for d in range(1, NY):
        w_y(d, lax.rem(y + NY - d, NY)).wait_recv()

    def w_x(d, column):
        to = device(lax.rem(x + d, NX), y, z, core)
        return remote(own_w.at[:, column], own_w.at[:, column], send_wx.at[d - 1], recv_wx.at[d - 1], to)

    for d in (2, 1, 3):
        w_x(d, x).start()

    for d in range(1, NY):
        y_copy(d, y).wait_recv()
    value = sums[y]
    for d in range(1, NY):
        value = value + sums_in[d - 1]
    total[...] = value.reshape(REDUCERS, 8, COLS)

    def z_copy(j, slot):
        to = device(x, y, core * HALF + 1 + j, core)
        return remote(total.at[j], total_in.at[slot], send_z.at[j], recv_z.at[slot], to)

    for j in range(REDUCERS):

        @pl.when(z != core * HALF + 1 + j)
        def _(j=j):
            z_copy(j, z).start()

    for d in range(1, NX):
        w_x(d, lax.rem(x + NX - d, NX)).wait_recv()
    w_c = remote(own_w, other_w, send_c.at[2], recv_c.at[2], sibling)
    w_c.start()
    weights = own_w[...].reshape(DH, COLS)
    kv[...] = jnp.dot(tok[:, pl.ds(mine, DH)], weights, preferred_element_type=F32)
    tgrad[core] = over_cols(cot[...], weights).astype(BF16)
    out_mine = pltpu.make_async_copy(tgrad.at[core], tokens_grad.at[:, pl.ds(mine, DH)], store_sem.at[0])
    out_mine.start()

    reducer = jnp.logical_and(home, jnp.logical_and(low >= 1, low <= REDUCERS))
    scale = F32(1.0 / math.sqrt(NX * NY * NZ * 2 * TOK))

    def g_copy(row, d):
        to = device(x, y, half * HALF + lax.rem(low + d, HALF), core)
        return remote(final.at[row], final.at[row], send_g.at[d - 1], recv_g.at[row], to)

    @pl.when(reducer)
    def _():
        for d in range(1, NZ):
            z_copy(0, lax.rem(z + d, NZ)).wait_recv()
        value = total[low - 1]
        for d in range(1, NZ):
            value = value + total_in[lax.rem(z + d, NZ)]
        final[low - 1] = value * scale
        for d in (3, 2, 4, 1, 5):
            g_copy(low - 1, d).start()

    w_c.wait_recv()
    weights = other_w[...].reshape(DH, COLS)
    both = kv[...] + jnp.dot(tok[:, pl.ds(theirs, DH)], weights, preferred_element_type=F32)
    tgrad[1 - core] = over_cols(cot[...], weights).astype(BF16)
    out_theirs = pltpu.make_async_copy(
        tgrad.at[1 - core], tokens_grad.at[:, pl.ds(theirs, DH)], store_sem.at[1]
    )
    out_theirs.start()
    kv_out = pl.ds(0, 256), pl.ds(256, 256)
    codes_kv = both.astype(BF16)
    cot2[...] = codes_kv
    out_keys = pltpu.make_async_copy(cot2.at[:, kv_out[0]], keys, store_sem.at[2])
    out_values = pltpu.make_async_copy(cot2.at[:, kv_out[1]], values, store_sem.at[3])
    out_keys.start()
    out_values.start()

    final_c = remote(final, final, send_c.at[3], recv_c.at[3], sibling)

    @pl.when(home)
    def _():
        for j in range(REDUCERS):

            @pl.when(low != 1 + j)
            def _(j=j):
                g_copy(j, 1).wait_recv()

        final_c.start()
        final_c.wait_send()

    @pl.when(jnp.logical_not(home))
    def _():
        final_c.wait_recv()

    for part_index, out in ((0, key_grad), (1, value_grad)):
        for j in range(REDUCERS):
            pltpu.make_async_copy(
                final.at[j, :, kv_out[part_index]], out.at[pl.ds(8 * j, 8)], store_sem.at[4 + part_index * 4 + j]
            ).start()

    swap_tok.wait_send()
    swap_cot.wait_send()

    @pl.when(home)
    def _():
        w_z.wait_send()

    for part_of in range(2):
        for d in range(1, NX):
            for copy in x_copies(part_of, d):
                copy.wait_send()
    for d in range(1, NY):
        w_y(d, y).wait_send()
        y_copy(d, y).wait_send()
    for d in range(1, NX):
        w_x(d, x).wait_send()
    w_c.wait_send()
    for j in range(REDUCERS):

        @pl.when(z != core * HALF + 1 + j)
        def _(j=j):
            z_copy(j, z).wait_send()

    @pl.when(reducer)
    def _():
        for d in range(1, HALF):
            g_copy(low - 1, d).wait_send()

    out_mine.wait()
    out_theirs.wait()
    out_keys.wait()
    out_values.wait()
    for part_index, out in ((0, key_grad), (1, value_grad)):
        for j in range(REDUCERS):
            pltpu.make_async_copy(
                final.at[j, :, kv_out[part_index]], out.at[pl.ds(8 * j, 8)], store_sem.at[4 + part_index * 4 + j]
            ).wait()


def on_device(tokens, key_cot, value_cot, key_mant, value_mant, key_expo, value_expo):
    dma, regular = pltpu.SemaphoreType.DMA, pltpu.SemaphoreType.REGULAR
    shape = jax.ShapeDtypeStruct
    anywhere = pl.BlockSpec(memory_space=pl.ANY)
    return pl.pallas_call(
        kernel,
        out_shape=(
            shape((TOK, 256), BF16),
            shape((TOK, 256), BF16),
            shape((TOK, 2 * DH), BF16),
            shape((ROWS, 256), F32),
            shape((ROWS, 256), F32),
        ),
        in_specs=[pl.BlockSpec(memory_space=pltpu.HBM)] * 7,
        out_specs=(anywhere,) * 5,
        scratch_shapes=[
            pltpu.VMEM((TOK, 2 * DH), BF16),
            pltpu.VMEM((TOK, DH), BF16),
            pltpu.VMEM((TOK, COLS), BF16),
            pltpu.VMEM((TOK, COLS), BF16),
            pltpu.VMEM((2, ROWS, 256), BF16),
            pltpu.VMEM((2, 2, ROWS), jnp.int32),
            pltpu.VMEM((NY, NX, ROWS, COLS), F32),
            pltpu.VMEM((NX - 1, NY, ROWS, COLS), I16),
            pltpu.VMEM((NX - 1, NY, 8, COLS), F32),
            pltpu.VMEM((NX - 1, NY, ROWS, COLS), I16),
            pltpu.VMEM((NX - 1, NY, 8, COLS), F32),
            pltpu.VMEM((NY, ROWS, COLS), F32),
            pltpu.VMEM((NY - 1, ROWS, COLS), F32),
            pltpu.VMEM((REDUCERS, 8, COLS), F32),
            pltpu.VMEM((NZ, 8, COLS), F32),
            pltpu.VMEM((REDUCERS, 8, COLS), F32),
            pltpu.VMEM((NY, NX, ROWS, COLS), BF16),
            pltpu.VMEM((NY, NX, ROWS, COLS), BF16),
            pltpu.VMEM((2, TOK, DH), BF16),
            pltpu.VMEM((TOK, COLS), F32),
            dma((7,)),
            dma((12,)),
            dma((4,)), dma((4,)),
            dma((2, 2, NX - 1)), dma((2, 2, NX - 1)),
            dma((NY - 1,)), dma((NY - 1,)),
            dma((REDUCERS,)), dma((NZ,)),
            dma((HALF - 1,)), dma((REDUCERS,)),
            dma, dma,
            dma((NY - 1,)), dma((NY - 1,)),
            dma((NX - 1,)), dma((NX - 1,)),
        ],
        compiler_params=pltpu.CompilerParams(
            collective_id=0, has_side_effects=True, vmem_limit_bytes=64 * 1024 * 1024
        ),
        name="projections",
    )(tokens, key_cot, value_cot, key_mant, value_mant, key_expo.T, value_expo.T)


def solution(mesh):
    rows, owned = P(("dp", "node"), None), P("node", None)
    return jax.shard_map(
        on_device,
        mesh=mesh,
        in_specs=(rows, rows, rows, owned, owned, owned, owned),
        out_specs=(rows, rows, rows, owned, owned),
        check_vma=False,
    )
```

time: 1760 us -> 75.9 us (0.04)
  the two profiles are of different devices: /device:TPU:1 before, /device:TPU:57 now
where the time goes in v1:
time: 75.9 us; the launch traced here: 75.6 us
  Pallas kernels  69 us (91%)
  local copies, waits for them, and re-layouts  5.96 us (8%)
    pallas_call x1, Pallas kernels, on_device(): pl.pallas_call(kernel, out_shape=(shape((TOK, 256), BF16), shape((TOK, 25...  69 us
    unnamed x11, local copies, waits for them, and re-layouts  5.96 us

profile of v1, /device:TPU:57, one launch (start us, length us, event | category | flops | bytes accessed | tf_op | source)
XLA Modules:
  0.0 75.6 jit_solution(13050544745600483873)
XLA Ops:
  0.6 69.0 %projections.1 = (bf16[256,256]{1,0:T(8,128)(2,1)}, bf16[256,256]{1,0:T(8,128)(2,1)}, bf16[256,2048]{1,0:T(8,128)(2,1)}, f32[32,256]{1,0:T(8,128)}, f32[32,256]{1,0:T(8,128)}) custom-call(bf16[256,2048]{1,0:T(8,128)(2,1)} %tokens.1, bf16[256,256]{1,0:T(8,128)(2,1)} %key_cot.1, bf16[256,256]{1,0:T(8,128)(2,1)} %value_cot.1, bf16[32,256]{1,0:T(8,128)(2,1)} %key_mant.1, ...), custom_call_target="tpu_custom_call" | custom-call | tf_op jit(solution)/shard_map/projections/pallas_call | solution.py:341
  69.6 0.0 copy-start
  69.6 1.6 %copy.17 = bf16[256,256]{1,0:T(8,128)(2,1)} copy(bf16[256,256]{1,0:T(8,128)(2,1)} %get-tuple-element.10) | data formatting | bytes 262144
  71.2 0.0 copy-done
  71.2 0.7 copy.18
  71.9 0.0 copy-start.2
  71.9 2.3 %copy.19 = bf16[256,2048]{1,0:T(8,128)(2,1)} copy(bf16[256,2048]{1,0:T(8,128)(2,1)} %get-tuple-element.12) | data formatting | bytes 2097152
  74.2 0.0 copy-done.2
  74.2 0.0 copy-start.1
  74.2 0.6 copy.20
  74.8 0.2 copy-done.1
  75.0 0.6 copy.21
Async XLA Ops:
  69.6 1.6 %copy-start = (bf16[256,256]{1,0:T(8,128)(2,1)S(1)}, bf16[256,256]{1,0:T(8,128)(2,1)}, u32[]{:S(2)}) copy-start(bf16[256,256]{1,0:T(8,128)(2,1)} %get-tuple-element.11) | copy-start | bytes 393220
  71.9 2.3 %copy-start.2 = (f32[32,256]{1,0:T(8,128)S(1)}, f32[32,256]{1,0:T(8,128)}, u32[]{:S(2)}) copy-start(f32[32,256]{1,0:T(8,128)} %get-tuple-element.13) | copy-start | bytes 98308
  74.2 0.8 %copy-start.1 = (f32[32,256]{1,0:T(8,128)S(1)}, f32[32,256]{1,0:T(8,128)}, u32[]{:S(2)}) copy-start(f32[32,256]{1,0:T(8,128)} %get-tuple-element.14) | copy-start | bytes 98308

commit v2 on v1

v2 whole, which is shorter than its diff:
```python
import math

import jax
import jax.numpy as jnp
from jax import lax
from jax.experimental import pallas as pl
from jax.experimental.pallas import tpu as pltpu
from jax.sharding import PartitionSpec as P

MESH = pl.DeviceIdType.MESH
F32, BF16, I16 = jnp.float32, jnp.bfloat16, jnp.int16
NX, NY, NZ = 4, 8, 12
HALF = NZ // 2
ROWS = 32
KVW = 256
COLS = 2 * KVW
TOK = 256
DH = 1024
REDUCERS = 4
STEPS = 32766.0
TINY = 1e-30


def coordinates():
    dp, node = lax.axis_index("dp"), lax.axis_index("node")
    x = lax.rem(node, NX)
    y = lax.rem(node // NX, NY)
    half = node // (NX * NY)
    low = dp // 2
    core = lax.rem(dp, 2)
    return x, y, half, low, core


def device(x, y, z, core):
    return {
        "dp": lax.rem(z, HALF) * 2 + core,
        "node": (z // HALF) * (NX * NY) + y * NX + x,
    }


def shard_rows(mant, expo_t):
    factor = jnp.zeros(expo_t.shape, F32)
    for exponent in range(-2, 2):
        factor = factor + jnp.where(expo_t == exponent, F32(2.0**exponent), F32(0.0))
    parts = []
    for block in range(2):
        spread = lax.dot_general(
            factor[block : block + 1, :],
            jnp.ones((1, 128), F32),
            (((0,), (0,)), ((), ())),
            preferred_element_type=F32,
        )
        parts.append(mant[:, block * 128 : (block + 1) * 128].astype(F32) * spread)
    return jnp.concatenate(parts, axis=1).astype(BF16)


def over_rows(left, right):
    return lax.dot_general(left, right, (((0,), (0,)), ((), ())), preferred_element_type=F32)


def over_cols(left, right):
    return lax.dot_general(left, right, (((1,), (1,)), ((), ())), preferred_element_type=F32)


def kernel(
    tokens, key_cot, value_cot, key_mant, value_mant, key_expo, value_expo,
    keys, values, tokens_grad, key_grad, value_grad,
    tok, tok2, cot, cot2, mant, expo, part, codes, peaks, codes_in, peaks_in,
    sums, sums_in, total, total_in, final, own_w, other_w, tgrad, kv, kv_out,
    load_sem, store_sem, send_c, recv_c, send_x, recv_x, send_y, recv_y,
    send_z, recv_z, send_g, recv_g, send_wz, recv_wz, send_wy, recv_wy, send_wx, recv_wx,
):
    x, y, half, low, core = coordinates()
    z = half * HALF + low
    sibling = device(x, y, z, 1 - core)
    home = core == half
    mine = pl.multiple_of(core * DH, DH)
    theirs = pl.multiple_of((1 - core) * DH, DH)

    def remote(src, dst, send, recv, to):
        return pltpu.make_async_remote_copy(
            src_ref=src, dst_ref=dst, send_sem=send, recv_sem=recv, device_id=to, device_id_type=MESH
        )

    loads = [
        pltpu.make_async_copy(key_mant, mant.at[0], load_sem.at[0]),
        pltpu.make_async_copy(value_mant, mant.at[1], load_sem.at[1]),
        pltpu.make_async_copy(key_expo, expo.at[0], load_sem.at[2]),
        pltpu.make_async_copy(value_expo, expo.at[1], load_sem.at[3]),
        pltpu.make_async_copy(tokens, tok, load_sem.at[4]),
        pltpu.make_async_copy(key_cot, cot.at[0], load_sem.at[5]),
        pltpu.make_async_copy(value_cot, cot.at[1], load_sem.at[6]),
    ]
    for load in loads:
        load.start()

    barrier = pltpu.get_barrier_semaphore()

    def greet(to):
        pl.semaphore_signal(barrier, inc=1, device_id=to, device_id_type=MESH)

    for d in (6, 5, 7, 4, 8, 3, 9, 2, 10, 1, 11):
        greet(device(x, y, lax.rem(z + d, NZ), core))
    for d in (4, 3, 5, 2, 6, 1, 7):
        greet(device(x, lax.rem(y + d, NY), z, core))
    for d in (2, 1, 3):
        greet(device(lax.rem(x + d, NX), y, z, core))
    greet(sibling)

    for load in loads[:4]:
        load.wait()

    @pl.when(home)
    def _():
        own_w[y, x, :, 0:KVW] = shard_rows(mant[0], expo[0])
        own_w[y, x, :, KVW:COLS] = shard_rows(mant[1], expo[1])

    for load in loads[4:]:
        load.wait()

    def own_part(b, _):
        left = tok[:, pl.ds(pl.multiple_of(b * 128, 128), 128)]
        part[b] = over_rows(left, cot[core]).reshape(NX, ROWS, KVW)
        return 0

    lax.fori_loop(0, 2 * NY, own_part, 0)
    pl.semaphore_wait(barrier, (NZ - 1) + (NY - 1) + (NX - 1) + 1)

    swap_cot = remote(cot.at[1 - core], cot2, send_c.at[0], recv_c.at[0], sibling)
    swaps = [
        remote(tok.at[:, pl.ds(h * DH, DH)], tok2.at[h], send_c.at[1 + h], recv_c.at[1 + h], sibling)
        for h in range(2)
    ]
    swap_cot.start()
    for swap in swaps:
        swap.start()

    across = device(x, y, lax.rem(z + HALF, NZ), core)
    w_z = remote(own_w.at[y, x], own_w.at[y, x], send_wz, recv_wz, across)

    @pl.when(home)
    def _():
        w_z.start()

    def x_copies(h, d):
        to = device(lax.rem(x + d, NX), y, z, core)
        return (
            remote(codes.at[h, d - 1], codes_in.at[h, d - 1],
                   send_x.at[0, h, d - 1], recv_x.at[0, h, d - 1], to),
            remote(peaks.at[h, d - 1], peaks_in.at[h, d - 1],
                   send_x.at[1, h, d - 1], recv_x.at[1, h, d - 1], to),
        )

    swap_cot.wait_recv()
    for h in range(2):
        swaps[h].wait_recv()

        def encode(j, _, h=h):
            left = tok2[h, :, pl.ds(pl.multiple_of(j * 128, 128), 128)]
            b = h * NY + j
            part[b] = part[b] + over_rows(left, cot2[...]).reshape(NX, ROWS, KVW)
            for d in range(1, NX):
                chunk = part[b, lax.rem(x + d, NX)]
                peak = jnp.maximum(jnp.max(jnp.abs(chunk), axis=0, keepdims=True), TINY)
                codes[h, d - 1, j] = jnp.round(chunk * (STEPS / peak)).astype(jnp.int32).astype(I16)
                peaks[h, d - 1, pl.ds(j, 1), :] = peak * (1.0 / STEPS)
            return 0

        lax.fori_loop(0, NY, encode, 0)
        for d in (2, 1, 3):
            for copy in x_copies(h, d):
                copy.start()

    @pl.when(jnp.logical_not(home))
    def _():
        w_z.wait_recv()

    def w_y(d, block):
        to = device(x, lax.rem(y + d, NY), z, core)
        return remote(own_w.at[block, x], own_w.at[block, x], send_wy.at[d - 1], recv_wy.at[d - 1], to)

    for d in (4, 3, 5, 2, 6, 1, 7):
        w_y(d, y).start()

    def y_copy(h, d, block):
        to = device(x, lax.rem(y + d, NY), z, core)
        return remote(sums.at[h, block], sums_in.at[h, d - 1], send_y.at[h, d - 1], recv_y.at[h, d - 1], to)

    for h in range(2):
        for d in (2, 1, 3):
            for copy in x_copies(h, d):
                copy.wait_recv()

        def add_x(j, _, h=h):
            value = part[h * NY + j, x]
            for d in range(1, NX):
                scale = peaks_in[h, d - 1, pl.ds(j, 1), :]
                value = value + codes_in[h, d - 1, j].astype(jnp.int32).astype(F32) * scale
            sums[h, j] = value
            return 0

        lax.fori_loop(0, NY, add_x, 0)
        for d in (4, 3, 5, 2, 6, 1, 7):
            y_copy(h, d, lax.rem(y + d, NY)).start()

    for d in range(1, NY):
        w_y(d, lax.rem(y + NY - d, NY)).wait_recv()

    def w_x(d, column):
        to = device(lax.rem(x + d, NX), y, z, core)
        return remote(own_w.at[:, column], own_w.at[:, column], send_wx.at[d - 1], recv_wx.at[d - 1], to)

    for d in (2, 1, 3):
        w_x(d, x).start()

    scale = F32(1.0 / math.sqrt(NX * NY * NZ * 2 * TOK))
    reducing = jnp.logical_and(low >= 1, low <= REDUCERS)

    def z_copy(h, j, slot):
        to = device(x, y, h * HALF + 1 + j, core)
        return remote(total.at[h, j], total_in.at[slot], send_z.at[h, j], recv_z.at[slot], to)

    def rows_of(j):
        return pl.ds(pl.multiple_of(8 * j, 8), 8)

    def g_copy(row, d):
        to = device(x, y, half * HALF + lax.rem(low + d, HALF), core)
        rows = final.at[core, rows_of(row)]
        return remote(rows, rows, send_g.at[d - 1], recv_g.at[row], to)

    def send_sums(h):
        for d in range(1, NY):
            y_copy(h, d, y).wait_recv()
        value = sums[h, y]
        for d in range(1, NY):
            value = value + sums_in[h, d - 1]
        total[h] = value.reshape(REDUCERS, 8, KVW)
        for j in range(REDUCERS):

            @pl.when(z != h * HALF + 1 + j)
            def _(j=j):
                z_copy(h, j, z).start()

    def reduce_sums(h):
        @pl.when(jnp.logical_and(half == h, reducing))
        def _():
            for d in range(1, NZ):
                z_copy(h, 0, lax.rem(z + d, NZ)).wait_recv()
            value = total[h, low - 1]
            for d in range(1, NZ):
                value = value + total_in[lax.rem(z + d, NZ)]
            final[core, rows_of(low - 1), :] = value * scale
            for d in (3, 2, 4, 1, 5):
                g_copy(low - 1, d).start()

    send_sums(0)
    reduce_sums(0)
    send_sums(1)

    for d in range(1, NX):
        w_x(d, lax.rem(x + NX - d, NX)).wait_recv()
    w_c = remote(own_w, other_w, send_c.at[3], recv_c.at[3], sibling)
    w_c.start()

    def products(weights, which, columns, store):
        grad = over_cols(cot[0], weights[:, 0:KVW]) + over_cols(cot[1], weights[:, KVW:COLS])
        tgrad[which] = grad.astype(BF16)
        out = pltpu.make_async_copy(tgrad.at[which], tokens_grad.at[:, pl.ds(columns, DH)], store_sem.at[store])
        out.start()
        return out, jnp.dot(tok[:, pl.ds(columns, DH)], weights, preferred_element_type=F32)

    out_mine, kv[...] = products(own_w[...].reshape(DH, COLS), core, mine, 0)
    reduce_sums(1)
    w_c.wait_recv()
    out_theirs, rest = products(other_w[...].reshape(DH, COLS), 1 - core, theirs, 1)
    kv_out[...] = (kv[...] + rest).astype(BF16)
    outs = [
        pltpu.make_async_copy(kv_out.at[:, pl.ds(0, KVW)], keys, store_sem.at[2]),
        pltpu.make_async_copy(kv_out.at[:, pl.ds(KVW, KVW)], values, store_sem.at[3]),
    ]
    for out in outs:
        out.start()

    for j in range(REDUCERS):

        @pl.when(low != 1 + j)
        def _(j=j):
            g_copy(j, 1).wait_recv()

    final_c = remote(final.at[core], final.at[core], send_c.at[4], recv_c.at[4], sibling)
    final_c.start()
    remote(final.at[1 - core], final.at[1 - core], send_c.at[4], recv_c.at[4], sibling).wait_recv()
    outs += [
        pltpu.make_async_copy(final.at[0], key_grad, store_sem.at[4]),
        pltpu.make_async_copy(final.at[1], value_grad, store_sem.at[5]),
    ]
    for out in outs[2:]:
        out.start()

    swap_cot.wait_send()
    for swap in swaps:
        swap.wait_send()

    @pl.when(home)
    def _():
        w_z.wait_send()

    for h in range(2):
        for d in range(1, NX):
            for copy in x_copies(h, d):
                copy.wait_send()
        for d in range(1, NY):
            y_copy(h, d, y).wait_send()
        for j in range(REDUCERS):

            @pl.when(z != h * HALF + 1 + j)
            def _(h=h, j=j):
                z_copy(h, j, z).wait_send()

    for d in range(1, NY):
        w_y(d, y).wait_send()
    for d in range(1, NX):
        w_x(d, x).wait_send()
    w_c.wait_send()

    @pl.when(reducing)
    def _():
        for d in range(1, HALF):
            g_copy(low - 1, d).wait_send()

    final_c.wait_send()
    out_mine.wait()
    out_theirs.wait()
    for out in outs:
        out.wait()


def place(*refs):
    sources, outs, staged, sems = refs[:5], refs[5:10], refs[10:15], refs[15]
    pieces = [(2, pl.ds(i * 64, 64)) for i in range(4)]
    pieces += [(i, pl.ds(0, sources[i].shape[0])) for i in (0, 1, 3, 4)]
    loads = [
        pltpu.make_async_copy(sources[i].at[rows], staged[i].at[rows], sems.at[0, k])
        for k, (i, rows) in enumerate(pieces)
    ]
    stores = [
        pltpu.make_async_copy(staged[i].at[rows], outs[i].at[rows], sems.at[1, k])
        for k, (i, rows) in enumerate(pieces)
    ]
    for load in loads:
        load.start()
    for load, store in zip(loads, stores):
        load.wait()
        store.start()
    for store in stores:
        store.wait()


def on_device(tokens, key_cot, value_cot, key_mant, value_mant, key_expo, value_expo):
    dma = pltpu.SemaphoreType.DMA
    shape = jax.ShapeDtypeStruct
    anywhere = pl.BlockSpec(memory_space=pl.ANY)
    results = (
        shape((TOK, KVW), BF16),
        shape((TOK, KVW), BF16),
        shape((TOK, 2 * DH), BF16),
        shape((ROWS, KVW), F32),
        shape((ROWS, KVW), F32),
    )
    outs = pl.pallas_call(
        kernel,
        out_shape=results,
        in_specs=[anywhere] * 7,
        out_specs=(anywhere,) * 5,
        scratch_shapes=[
            pltpu.VMEM((TOK, 2 * DH), BF16),
            pltpu.VMEM((2, TOK, DH), BF16),
            pltpu.VMEM((2, TOK, KVW), BF16),
            pltpu.VMEM((TOK, KVW), BF16),
            pltpu.VMEM((2, ROWS, KVW), BF16),
            pltpu.VMEM((2, 2, ROWS), jnp.int32),
            pltpu.VMEM((2 * NY, NX, ROWS, KVW), F32),
            pltpu.VMEM((2, NX - 1, NY, ROWS, KVW), I16),
            pltpu.VMEM((2, NX - 1, NY, KVW), F32),
            pltpu.VMEM((2, NX - 1, NY, ROWS, KVW), I16),
            pltpu.VMEM((2, NX - 1, NY, KVW), F32),
            pltpu.VMEM((2, NY, ROWS, KVW), F32),
            pltpu.VMEM((2, NY - 1, ROWS, KVW), F32),
            pltpu.VMEM((2, REDUCERS, 8, KVW), F32),
            pltpu.VMEM((NZ, 8, KVW), F32),
            pltpu.VMEM((2, ROWS, KVW), F32),
            pltpu.VMEM((NY, NX, ROWS, COLS), BF16),
            pltpu.VMEM((NY, NX, ROWS, COLS), BF16),
            pltpu.VMEM((2, TOK, DH), BF16),
            pltpu.VMEM((TOK, COLS), F32),
            pltpu.VMEM((TOK, COLS), BF16),
            dma((7,)),
            dma((6,)),
            dma((5,)), dma((5,)),
            dma((2, 2, NX - 1)), dma((2, 2, NX - 1)),
            dma((2, NY - 1)), dma((2, NY - 1)),
            dma((2, REDUCERS)), dma((NZ,)),
            dma((HALF - 1,)), dma((REDUCERS,)),
            dma, dma,
            dma((NY - 1,)), dma((NY - 1,)),
            dma((NX - 1,)), dma((NX - 1,)),
        ],
        compiler_params=pltpu.CompilerParams(
            collective_id=0, has_side_effects=True, vmem_limit_bytes=64 * 1024 * 1024
        ),
        name="projections",
    )(tokens, key_cot, value_cot, key_mant, value_mant, key_expo.T, value_expo.T)
    return pl.pallas_call(
        place,
        out_shape=results,
        in_specs=[anywhere] * 5,
        out_specs=(anywhere,) * 5,
        scratch_shapes=[pltpu.VMEM(r.shape, r.dtype) for r in results] + [dma((2, 8))],
        compiler_params=pltpu.CompilerParams(vmem_limit_bytes=64 * 1024 * 1024),
        name="place",
    )(*outs)


def solution(mesh):
    rows, owned = P(("dp", "node"), None), P("node", None)
    return jax.shard_map(
        on_device,
        mesh=mesh,
        in_specs=(rows, rows, rows, owned, owned, owned, owned),
        out_specs=(rows, rows, rows, owned, owned),
        check_vma=False,
    )
```

time: 75.9 us -> 58.5 us (0.77)
  the two profiles are of different devices: /device:TPU:57 before, /device:TPU:1 now
where the time goes in v2:
time: 58.5 us; the launch traced here: 58.3 us
  Pallas kernels  57.7 us (99%)
  between operations  0.64 us (1%)
    pallas_call x1, Pallas kernels, on_device(): pl.pallas_call(kernel, out_shape=results, in_specs=[anywhere] * 7, out_sp...  55.5 us
    pallas_call x1, Pallas kernels, on_device(): pl.pallas_call(place, out_shape=results, in_specs=[anywhere] * 5, out_spe...  2.15 us

profile of v2, /device:TPU:1, one launch (start us, length us, event | category | flops | bytes accessed | tf_op | source)
XLA Modules:
  0.0 58.3 jit_solution(1779326984020850030)
XLA Ops:
  0.6 55.5 %projections.1 = (bf16[256,256]{1,0:T(8,128)(2,1)}, bf16[256,256]{1,0:T(8,128)(2,1)}, bf16[256,2048]{1,0:T(8,128)(2,1)}, f32[32,256]{1,0:T(8,128)}, f32[32,256]{1,0:T(8,128)}) custom-call(bf16[256,2048]{1,0:T(8,128)(2,1)} %tokens.1, bf16[256,256]{1,0:T(8,128)(2,1)} %key_cot.1, bf16[256,256]{1,0:T(8,128)(2,1)} %value_cot.1, bf16[32,256]{1,0:T(8,128)(2,1)} %key_mant.1, ...), custom_call_target="tpu_custom_call" | custom-call | tf_op jit(solution)/shard_map/projections/pallas_call | solution.py:370
  56.2 2.1 %place.1 = (bf16[256,256]{1,0:T(8,128)(2,1)}, bf16[256,256]{1,0:T(8,128)(2,1)}, bf16[256,2048]{1,0:T(8,128)(2,1)}, f32[32,256]{1,0:T(8,128)}, f32[32,256]{1,0:T(8,128)}) custom-call(bf16[256,256]{1,0:T(8,128)(2,1)} %get-tuple-element.10.refs_0_, bf16[256,256]{1,0:T(8,128)(2,1)} %get-tuple-element.11.refs_1_, bf16[256,2048]{1,0:T(8,128)(2,1)} %get-tuple-element.12.refs_2_, ...), custom_call_target="tpu_custom_call" | custom-call | tf_op jit(solution)/shard_map/place/pallas_call | solution.py:413

commit v3 on v2

--- a/solution.py
+++ b/solution.py
@@ -68,7 +68,7 @@
     tok, tok2, cot, cot2, mant, expo, part, codes, peaks, codes_in, peaks_in,
     sums, sums_in, total, total_in, final, own_w, other_w, tgrad, kv, kv_out,
     load_sem, store_sem, send_c, recv_c, send_x, recv_x, send_y, recv_y,
-    send_z, recv_z, send_g, recv_g, send_wz, recv_wz, send_wy, recv_wy, send_wx, recv_wx,
+    send_z, recv_z, send_g, recv_g, answered, send_wz, recv_wz, send_wy, recv_wy, send_wx, recv_wx,
 ):
     x, y, half, low, core = coordinates()
     z = half * HALF + low
@@ -99,8 +99,12 @@
     def greet(to):
         pl.semaphore_signal(barrier, inc=1, device_id=to, device_id_type=MESH)
 
-    for d in (6, 5, 7, 4, 8, 3, 9, 2, 10, 1, 11):
-        greet(device(x, y, lax.rem(z + d, NZ), core))
+    for d in range(NZ - 1, 0, -1):
+
+        @pl.when(z + d < NZ)
+        def _(d=d):
+            greet(device(x, y, z + d, core))
+
     for d in (4, 3, 5, 2, 6, 1, 7):
         greet(device(x, lax.rem(y + d, NY), z, core))
     for d in (2, 1, 3):
@@ -124,7 +128,20 @@
         return 0
 
     lax.fori_loop(0, 2 * NY, own_part, 0)
-    pl.semaphore_wait(barrier, (NZ - 1) + (NY - 1) + (NX - 1) + 1)
+    pl.semaphore_wait(barrier, z + (NY - 1) + (NX - 1) + 1)
+    for d in range(NZ - 1, 0, -1):
+
+        @pl.when(z >= d)
+        def _(d=d):
+            pl.semaphore_signal(
+                answered, inc=1, device_id=device(x, y, z - d, core), device_id_type=MESH
+            )
+
+    def wait_answers():
+        @pl.when(z < NZ - 1)
+        def _():
+            pl.semaphore_wait(answered, NZ - 1 - z)
+
 
     swap_cot = remote(cot.at[1 - core], cot2, send_c.at[0], recv_c.at[0], sibling)
     swaps = [
@@ -135,12 +152,20 @@
     for swap in swaps:
         swap.start()
 
-    across = device(x, y, lax.rem(z + HALF, NZ), core)
-    w_z = remote(own_w.at[y, x], own_w.at[y, x], send_wz, recv_wz, across)
-
-    @pl.when(home)
-    def _():
-        w_z.start()
+    edge = jnp.logical_or(low == 0, low == HALF - 1)
+    outward = 2 * (low // (HALF - 1)) - 1
+
+    def w_z(k):
+        to = device(x, y, lax.rem(z + NZ + outward * k, NZ), core)
+        return remote(own_w.at[y, x], own_w.at[y, x], send_wz.at[k - 1], recv_wz, to)
+
+    def send_shard(of):
+        @pl.when(jnp.logical_and(jnp.logical_and(home, edge), half == of))
+        def _():
+            for k in (3, 2, 1):
+                w_z(k).start()
+
+    send_shard(1)
 
     def x_copies(h, d):
         to = device(lax.rem(x + d, NX), y, z, core)
@@ -171,9 +196,15 @@
             for copy in x_copies(h, d):
                 copy.start()
 
+    @pl.when(edge)
+    def _():
+        wait_answers()
+
+    send_shard(0)
+
     @pl.when(jnp.logical_not(home))
     def _():
-        w_z.wait_recv()
+        w_z(1).wait_recv()
 
     def w_y(d, block):
         to = device(x, lax.rem(y + d, NY), z, core)
@@ -214,10 +245,10 @@
         w_x(d, x).start()
 
     scale = F32(1.0 / math.sqrt(NX * NY * NZ * 2 * TOK))
-    reducing = jnp.logical_and(low >= 1, low <= REDUCERS)
+    reducing = low < REDUCERS
 
     def z_copy(h, j, slot):
-        to = device(x, y, h * HALF + 1 + j, core)
+        to = device(x, y, h * HALF + j, core)
         return remote(total.at[h, j], total_in.at[slot], send_z.at[h, j], recv_z.at[slot], to)
 
     def rows_of(j):
@@ -237,7 +268,7 @@
         total[h] = value.reshape(REDUCERS, 8, KVW)
         for j in range(REDUCERS):
 
-            @pl.when(z != h * HALF + 1 + j)
+            @pl.when(z != h * HALF + j)
             def _(j=j):
                 z_copy(h, j, z).start()
 
@@ -246,12 +277,16 @@
         def _():
             for d in range(1, NZ):
                 z_copy(h, 0, lax.rem(z + d, NZ)).wait_recv()
-            value = total[h, low - 1]
+            value = total[h, low]
             for d in range(1, NZ):
                 value = value + total_in[lax.rem(z + d, NZ)]
-            final[core, rows_of(low - 1), :] = value * scale
+            final[core, rows_of(low), :] = value * scale
             for d in (3, 2, 4, 1, 5):
-                g_copy(low - 1, d).start()
+                g_copy(low, d).start()
+
+    @pl.when(jnp.logical_not(edge))
+    def _():
+        wait_answers()
 
     send_sums(0)
     reduce_sums(0)
@@ -283,7 +318,7 @@
 
     for j in range(REDUCERS):
 
-        @pl.when(low != 1 + j)
+        @pl.when(low != j)
         def _(j=j):
             g_copy(j, 1).wait_recv()
 
@@ -301,9 +336,10 @@
     for swap in swaps:
         swap.wait_send()
 
-    @pl.when(home)
-    def _():
-        w_z.wait_send()
+    @pl.when(jnp.logical_and(home, edge))
+    def _():
+        for k in (1, 2, 3):
+            w_z(k).wait_send()
 
     for h in range(2):
         for d in range(1, NX):
@@ -313,7 +349,7 @@
             y_copy(h, d, y).wait_send()
         for j in range(REDUCERS):
 
-            @pl.when(z != h * HALF + 1 + j)
+            @pl.when(z != h * HALF + j)
             def _(h=h, j=j):
                 z_copy(h, j, z).wait_send()
 
@@ -326,7 +362,7 @@
     @pl.when(reducing)
     def _():
         for d in range(1, HALF):
-            g_copy(low - 1, d).wait_send()
+            g_copy(low, d).wait_send()
 
     final_c.wait_send()
     out_mine.wait()
@@ -401,7 +437,8 @@
             dma((2, NY - 1)), dma((2, NY - 1)),
             dma((2, REDUCERS)), dma((NZ,)),
             dma((HALF - 1,)), dma((REDUCERS,)),
-            dma, dma,
+            pltpu.SemaphoreType.REGULAR,
+            dma((3,)), dma,
             dma((NY - 1,)), dma((NY - 1,)),
             dma((NX - 1,)), dma((NX - 1,)),
         ],

time: 58.5 us -> 56.8 us (0.971)
  Pallas kernels: 57.7 us -> 56 us
    pallas_call x1, Pallas kernels: 55.5 us -> 53.9 us  [on_device(): pl.pallas_call(kernel, out_shape=results, in_specs=[anywhere] * 7, out_sp...]
where the time goes in v3:
time: 56.8 us; the launch traced here: 56.6 us
  Pallas kernels  56 us (99%)
  between operations  0.64 us (1%)
    pallas_call x1, Pallas kernels, on_device(): pl.pallas_call(kernel, out_shape=results, in_specs=[anywhere] * 7, out_sp...  53.9 us
    pallas_call x1, Pallas kernels, on_device(): pl.pallas_call(place, out_shape=results, in_specs=[anywhere] * 5, out_spe...  2.15 us

profile of v3, /device:TPU:1, one launch (start us, length us, event | category | flops | bytes accessed | tf_op | source)
XLA Modules:
  0.0 56.6 jit_solution(16367257053488501303)
XLA Ops:
  0.6 53.9 %projections.1 = (bf16[256,256]{1,0:T(8,128)(2,1)}, bf16[256,256]{1,0:T(8,128)(2,1)}, bf16[256,2048]{1,0:T(8,128)(2,1)}, f32[32,256]{1,0:T(8,128)}, f32[32,256]{1,0:T(8,128)}) custom-call(bf16[256,2048]{1,0:T(8,128)(2,1)} %tokens.1, bf16[256,256]{1,0:T(8,128)(2,1)} %key_cot.1, bf16[256,256]{1,0:T(8,128)(2,1)} %value_cot.1, bf16[32,256]{1,0:T(8,128)(2,1)} %key_mant.1, ...), custom_call_target="tpu_custom_call" | custom-call | tf_op jit(solution)/shard_map/projections/pallas_call | solution.py:406
  54.5 2.1 %place.1 = (bf16[256,256]{1,0:T(8,128)(2,1)}, bf16[256,256]{1,0:T(8,128)(2,1)}, bf16[256,2048]{1,0:T(8,128)(2,1)}, f32[32,256]{1,0:T(8,128)}, f32[32,256]{1,0:T(8,128)}) custom-call(bf16[256,256]{1,0:T(8,128)(2,1)} %get-tuple-element.10.refs_0_, bf16[256,256]{1,0:T(8,128)(2,1)} %get-tuple-element.11.refs_1_, bf16[256,2048]{1,0:T(8,128)(2,1)} %get-tuple-element.12.refs_2_, ...), custom_call_target="tpu_custom_call" | custom-call | tf_op jit(solution)/shard_map/place/pallas_call | solution.py:450

commit v4 on v3

--- a/solution.py
+++ b/solution.py
@@ -66,7 +66,7 @@
     tokens, key_cot, value_cot, key_mant, value_mant, key_expo, value_expo,
     keys, values, tokens_grad, key_grad, value_grad,
     tok, tok2, cot, cot2, mant, expo, part, codes, peaks, codes_in, peaks_in,
-    sums, sums_in, total, total_in, final, own_w, other_w, tgrad, kv, kv_out,
+    sums, codes_y, peaks_y, codes_y_in, peaks_y_in, total, total_in, final, own_w, other_w, tgrad, kv, kv_out,
     load_sem, store_sem, send_c, recv_c, send_x, recv_x, send_y, recv_y,
     send_z, recv_z, send_g, recv_g, answered, send_wz, recv_wz, send_wy, recv_wy, send_wx, recv_wx,
 ):
@@ -122,12 +122,15 @@
     for load in loads[4:]:
         load.wait()
 
-    def own_part(b, _):
+    def own_part(b):
         left = tok[:, pl.ds(pl.multiple_of(b * 128, 128), 128)]
-        part[b] = over_rows(left, cot[core]).reshape(NX, ROWS, KVW)
+        return over_rows(left, cot[core]).reshape(NX, ROWS, KVW)
+
+    def first_part(b, _):
+        part[b] = own_part(b)
         return 0
 
-    lax.fori_loop(0, 2 * NY, own_part, 0)
+    lax.fori_loop(0, NY, first_part, 0)
     pl.semaphore_wait(barrier, z + (NY - 1) + (NX - 1) + 1)
     for d in range(NZ - 1, 0, -1):
 
@@ -149,8 +152,7 @@
         for h in range(2)
     ]
     swap_cot.start()
-    for swap in swaps:
-        swap.start()
+    swaps[0].start()
 
     edge = jnp.logical_or(low == 0, low == HALF - 1)
     outward = 2 * (low // (HALF - 1)) - 1
@@ -176,25 +178,39 @@
                    send_x.at[1, h, d - 1], recv_x.at[1, h, d - 1], to),
         )
 
+    def coded(chunk):
+        peak = jnp.maximum(jnp.max(jnp.abs(chunk), axis=0, keepdims=True), TINY)
+        codes_of = jnp.round(chunk * (STEPS / peak)).astype(jnp.int32).astype(I16)
+        return codes_of, peak * (1.0 / STEPS)
+
+    def decoded(codes_of, scales):
+        return codes_of.astype(jnp.int32).astype(F32) * scales
+
     swap_cot.wait_recv()
     for h in range(2):
         swaps[h].wait_recv()
-
-        def encode(j, _, h=h):
+        if h == 0:
+            swaps[1].start()
+
+        def both_parts(j, _, h=h):
             left = tok2[h, :, pl.ds(pl.multiple_of(j * 128, 128), 128)]
             b = h * NY + j
-            part[b] = part[b] + over_rows(left, cot2[...]).reshape(NX, ROWS, KVW)
-            for d in range(1, NX):
-                chunk = part[b, lax.rem(x + d, NX)]
-                peak = jnp.maximum(jnp.max(jnp.abs(chunk), axis=0, keepdims=True), TINY)
-                codes[h, d - 1, j] = jnp.round(chunk * (STEPS / peak)).astype(jnp.int32).astype(I16)
-                peaks[h, d - 1, pl.ds(j, 1), :] = peak * (1.0 / STEPS)
+            first = part[b] if h == 0 else own_part(b)
+            part[b] = first + over_rows(left, cot2[...]).reshape(NX, ROWS, KVW)
             return 0
 
-        lax.fori_loop(0, NY, encode, 0)
+        lax.fori_loop(0, NY, both_parts, 0)
         for d in (2, 1, 3):
-            for copy in x_copies(h, d):
-                copy.start()
+
+            def encode(j, _, h=h, d=d):
+                codes[h, d - 1, j], scales = coded(part[h * NY + j, lax.rem(x + d, NX)])
+                peaks[h, d - 1, pl.ds(j, 1), :] = scales
+                return 0
+
+            lax.fori_loop(0, NY, encode, 0)
+            if h == 0:
+                for copy in x_copies(0, d):
+                    copy.start()
 
     @pl.when(edge)
     def _():
@@ -213,27 +229,49 @@
     for d in (4, 3, 5, 2, 6, 1, 7):
         w_y(d, y).start()
 
-    def y_copy(h, d, block):
+    for d in (2, 1, 3):
+        for copy in x_copies(0, d):
+            copy.wait_send()
+    for d in (2, 1, 3):
+        for copy in x_copies(1, d):
+            copy.start()
+
+    def y_copies(h, d, block):
         to = device(x, lax.rem(y + d, NY), z, core)
-        return remote(sums.at[h, block], sums_in.at[h, d - 1], send_y.at[h, d - 1], recv_y.at[h, d - 1], to)
-
-    for h in range(2):
+        return (
+            remote(codes_y.at[h, block], codes_y_in.at[h, d - 1],
+                   send_y.at[0, h, d - 1], recv_y.at[0, h, d - 1], to),
+            remote(peaks_y.at[h, block], peaks_y_in.at[h, d - 1],
+                   send_y.at[1, h, d - 1], recv_y.at[1, h, d - 1], to),
+        )
+
+    def sum_x(h):
         for d in (2, 1, 3):
             for copy in x_copies(h, d):
                 copy.wait_recv()
 
-        def add_x(j, _, h=h):
-            value = part[h * NY + j, x]
+        def add_x(block):
+            value = part[h * NY + block, x]
             for d in range(1, NX):
-                scale = peaks_in[h, d - 1, pl.ds(j, 1), :]
-                value = value + codes_in[h, d - 1, j].astype(jnp.int32).astype(F32) * scale
-            sums[h, j] = value
+                value = value + decoded(codes_in[h, d - 1, block], peaks_in[h, d - 1, pl.ds(block, 1), :])
+            return value
+
+        def add_and_send(i, _):
+            d = NY // 2 + (1 - 2 * lax.rem(i, 2)) * ((i + 1) // 2)
+            block = lax.rem(y + d, NY)
+            codes_y[h, block], peaks_y[h, block] = coded(add_x(block))
+            for copy in y_copies(h, d, block):
+                copy.start()
             return 0
 
-        lax.fori_loop(0, NY, add_x, 0)
-        for d in (4, 3, 5, 2, 6, 1, 7):
-            y_copy(h, d, lax.rem(y + d, NY)).start()
-
+        lax.fori_loop(0, NY - 1, add_and_send, 0)
+        sums[h] = add_x(y)
+
+    sum_x(0)
+
+    for d in (2, 1, 3):
+        for copy in x_copies(1, d):
+            copy.wait_send()
     for d in range(1, NY):
         w_y(d, lax.rem(y + NY - d, NY)).wait_recv()
 
@@ -261,10 +299,11 @@
 
     def send_sums(h):
         for d in range(1, NY):
-            y_copy(h, d, y).wait_recv()
-        value = sums[h, y]
+            for copy in y_copies(h, d, y):
+                copy.wait_recv()
+        value = sums[h]
         for d in range(1, NY):
-            value = value + sums_in[h, d - 1]
+            value = value + decoded(codes_y_in[h, d - 1], peaks_y_in[h, d - 1])
         total[h] = value.reshape(REDUCERS, 8, KVW)
         for j in range(REDUCERS):
 
@@ -289,8 +328,9 @@
         wait_answers()
 
     send_sums(0)
+    sum_x(1)
+    send_sums(1)
     reduce_sums(0)
-    send_sums(1)
 
     for d in range(1, NX):
         w_x(d, lax.rem(x + NX - d, NX)).wait_recv()
@@ -342,11 +382,9 @@
             w_z(k).wait_send()
 
     for h in range(2):
-        for d in range(1, NX):
-            for copy in x_copies(h, d):
+        for d in range(1, NY):
+            for copy in y_copies(h, d, y):
                 copy.wait_send()
-        for d in range(1, NY):
-            y_copy(h, d, y).wait_send()
         for j in range(REDUCERS):
 
             @pl.when(z != h * HALF + j)
@@ -420,8 +458,11 @@
             pltpu.VMEM((2, NX - 1, NY, KVW), F32),
             pltpu.VMEM((2, NX - 1, NY, ROWS, KVW), I16),
             pltpu.VMEM((2, NX - 1, NY, KVW), F32),
-            pltpu.VMEM((2, NY, ROWS, KVW), F32),
-            pltpu.VMEM((2, NY - 1, ROWS, KVW), F32),
+            pltpu.VMEM((2, ROWS, KVW), F32),
+            pltpu.VMEM((2, NY, ROWS, KVW), I16),
+            pltpu.VMEM((2, NY, 1, KVW), F32),
+            pltpu.VMEM((2, NY - 1, ROWS, KVW), I16),
+            pltpu.VMEM((2, NY - 1, 1, KVW), F32),
             pltpu.VMEM((2, REDUCERS, 8, KVW), F32),
             pltpu.VMEM((NZ, 8, KVW), F32),
             pltpu.VMEM((2, ROWS, KVW), F32),
@@ -434,7 +475,7 @@
             dma((6,)),
             dma((5,)), dma((5,)),
             dma((2, 2, NX - 1)), dma((2, 2, NX - 1)),
-            dma((2, NY - 1)), dma((2, NY - 1)),
+            dma((2, 2, NY - 1)), dma((2, 2, NY - 1)),
             dma((2, REDUCERS)), dma((NZ,)),
             dma((HALF - 1,)), dma((REDUCERS,)),
             pltpu.SemaphoreType.REGULAR,

time: 56.8 us -> 54 us (0.951)
  Pallas kernels: 56 us -> 53.2 us
    pallas_call x1, Pallas kernels: 53.9 us -> 51 us  [on_device(): pl.pallas_call(kernel, out_shape=results, in_specs=[anywhere] * 7, out_sp...]
where the time goes in v4:
time: 54 us; the launch traced here: 53.8 us
  Pallas kernels  53.2 us (99%)
  between operations  0.64 us (1%)
    pallas_call x1, Pallas kernels, on_device(): pl.pallas_call(kernel, out_shape=results, in_specs=[anywhere] * 7, out_sp...  51 us
    pallas_call x1, Pallas kernels, on_device(): pl.pallas_call(place, out_shape=results, in_specs=[anywhere] * 5, out_spe...  2.15 us

profile of v4, /device:TPU:1, one launch (start us, length us, event | category | flops | bytes accessed | tf_op | source)
XLA Modules:
  0.0 53.8 jit_solution(15382155955497176907)
XLA Ops:
  0.6 51.0 %projections.1 = (bf16[256,256]{1,0:T(8,128)(2,1)}, bf16[256,256]{1,0:T(8,128)(2,1)}, bf16[256,2048]{1,0:T(8,128)(2,1)}, f32[32,256]{1,0:T(8,128)}, f32[32,256]{1,0:T(8,128)}) custom-call(bf16[256,2048]{1,0:T(8,128)(2,1)} %tokens.1, bf16[256,256]{1,0:T(8,128)(2,1)} %key_cot.1, bf16[256,256]{1,0:T(8,128)(2,1)} %value_cot.1, bf16[32,256]{1,0:T(8,128)(2,1)} %key_mant.1, ...), custom_call_target="tpu_custom_call" | custom-call | tf_op jit(solution)/shard_map/projections/pallas_call | solution.py:444
  51.7 2.1 %place.1 = (bf16[256,256]{1,0:T(8,128)(2,1)}, bf16[256,256]{1,0:T(8,128)(2,1)}, bf16[256,2048]{1,0:T(8,128)(2,1)}, f32[32,256]{1,0:T(8,128)}, f32[32,256]{1,0:T(8,128)}) custom-call(bf16[256,256]{1,0:T(8,128)(2,1)} %get-tuple-element.10.refs_0_, bf16[256,256]{1,0:T(8,128)(2,1)} %get-tuple-element.11.refs_1_, bf16[256,2048]{1,0:T(8,128)(2,1)} %get-tuple-element.12.refs_2_, ...), custom_call_target="tpu_custom_call" | custom-call | tf_op jit(solution)/shard_map/place/pallas_call | solution.py:491

commit v5 on v4

--- a/solution.py
+++ b/solution.py
@@ -62,6 +62,18 @@
     return lax.dot_general(left, right, (((1,), (1,)), ((), ())), preferred_element_type=F32)
 
 
+def each(count, step):
+    def body(i, _):
+        step(i)
+        return 0
+
+    lax.fori_loop(0, count, body, 0)
+
+
+def around(i, ring):
+    return ring // 2 + (1 - 2 * lax.rem(i, 2)) * ((i + 1) // 2)
+
+
 def kernel(
     tokens, key_cot, value_cot, key_mant, value_mant, key_expo, value_expo,
     keys, values, tokens_grad, key_grad, value_grad,
@@ -74,8 +86,6 @@
     z = half * HALF + low
     sibling = device(x, y, z, 1 - core)
     home = core == half
-    mine = pl.multiple_of(core * DH, DH)
-    theirs = pl.multiple_of((1 - core) * DH, DH)
 
     def remote(src, dst, send, recv, to):
         return pltpu.make_async_remote_copy(
@@ -91,7 +101,7 @@
         pltpu.make_async_copy(key_cot, cot.at[0], load_sem.at[5]),
         pltpu.make_async_copy(value_cot, cot.at[1], load_sem.at[6]),
     ]
-    for load in loads:
+    for load in loads[4:] + loads[:4]:
         load.start()
 
     barrier = pltpu.get_barrier_semaphore()
@@ -99,25 +109,10 @@
     def greet(to):
         pl.semaphore_signal(barrier, inc=1, device_id=to, device_id_type=MESH)
 
-    for d in range(NZ - 1, 0, -1):
-
-        @pl.when(z + d < NZ)
-        def _(d=d):
-            greet(device(x, y, z + d, core))
-
-    for d in (4, 3, 5, 2, 6, 1, 7):
-        greet(device(x, lax.rem(y + d, NY), z, core))
-    for d in (2, 1, 3):
-        greet(device(lax.rem(x + d, NX), y, z, core))
+    each(NY - 1, lambda i: greet(device(x, lax.rem(y + around(i, NY), NY), z, core)))
+    each(NX - 1, lambda i: greet(device(lax.rem(x + around(i, NX), NX), y, z, core)))
     greet(sibling)
-
-    for load in loads[:4]:
-        load.wait()
-
-    @pl.when(home)
-    def _():
-        own_w[y, x, :, 0:KVW] = shard_rows(mant[0], expo[0])
-        own_w[y, x, :, KVW:COLS] = shard_rows(mant[1], expo[1])
+    each(NZ - 1 - z, lambda i: greet(device(x, y, NZ - 1 - i, core)))
 
     for load in loads[4:]:
         load.wait()
@@ -132,13 +127,12 @@
 
     lax.fori_loop(0, NY, first_part, 0)
     pl.semaphore_wait(barrier, z + (NY - 1) + (NX - 1) + 1)
-    for d in range(NZ - 1, 0, -1):
-
-        @pl.when(z >= d)
-        def _(d=d):
-            pl.semaphore_signal(
-                answered, inc=1, device_id=device(x, y, z - d, core), device_id_type=MESH
-            )
+    each(
+        z,
+        lambda i: pl.semaphore_signal(
+            answered, inc=1, device_id=device(x, y, i, core), device_id_type=MESH
+        ),
+    )
 
     def wait_answers():
         @pl.when(z < NZ - 1)
@@ -154,6 +148,14 @@
     swap_cot.start()
     swaps[0].start()
 
+    for load in loads[:4]:
+        load.wait()
+
+    @pl.when(home)
+    def _():
+        own_w[y, x, :, 0:KVW] = shard_rows(mant[0], expo[0])
+        own_w[y, x, :, KVW:COLS] = shard_rows(mant[1], expo[1])
+
     edge = jnp.logical_or(low == 0, low == HALF - 1)
     outward = 2 * (low // (HALF - 1)) - 1
 
@@ -164,8 +166,7 @@
     def send_shard(of):
         @pl.when(jnp.logical_and(jnp.logical_and(home, edge), half == of))
         def _():
-            for k in (3, 2, 1):
-                w_z(k).start()
+            each(HALF // 2, lambda i: w_z(HALF // 2 - i).start())
 
     send_shard(1)
 
@@ -200,18 +201,20 @@
             return 0
 
         lax.fori_loop(0, NY, both_parts, 0)
-        for d in (2, 1, 3):
-
-            def encode(j, _, h=h, d=d):
+        def encode_for(i, h=h):
+            d = around(i, NX)
+
+            def encode(j):
                 codes[h, d - 1, j], scales = coded(part[h * NY + j, lax.rem(x + d, NX)])
                 peaks[h, d - 1, pl.ds(j, 1), :] = scales
-                return 0
-
-            lax.fori_loop(0, NY, encode, 0)
+
+            each(NY, encode)
             if h == 0:
                 for copy in x_copies(0, d):
                     copy.start()
 
+        each(NX - 1, encode_for)
+
     @pl.when(edge)
     def _():
         wait_answers()
@@ -226,15 +229,18 @@
         to = device(x, lax.rem(y + d, NY), z, core)
         return remote(own_w.at[block, x], own_w.at[block, x], send_wy.at[d - 1], recv_wy.at[d - 1], to)
 
-    for d in (4, 3, 5, 2, 6, 1, 7):
-        w_y(d, y).start()
-
-    for d in (2, 1, 3):
-        for copy in x_copies(0, d):
+    each(NY - 1, lambda i: w_y(around(i, NY), y).start())
+
+    def wait_sent_x(i, h):
+        for copy in x_copies(h, i + 1):
             copy.wait_send()
-    for d in (2, 1, 3):
-        for copy in x_copies(1, d):
+
+    def start_x(i):
+        for copy in x_copies(1, around(i, NX)):
             copy.start()
+
+    each(NX - 1, lambda i: wait_sent_x(i, 0))
+    each(NX - 1, start_x)
 
     def y_copies(h, d, block):
         to = device(x, lax.rem(y + d, NY), z, core)
@@ -246,9 +252,11 @@
         )
 
     def sum_x(h):
-        for d in (2, 1, 3):
-            for copy in x_copies(h, d):
+        def wait_x(i):
+            for copy in x_copies(h, i + 1):
                 copy.wait_recv()
+
+        each(NX - 1, wait_x)
 
         def add_x(block):
             value = part[h * NY + block, x]
@@ -256,31 +264,26 @@
                 value = value + decoded(codes_in[h, d - 1, block], peaks_in[h, d - 1, pl.ds(block, 1), :])
             return value
 
-        def add_and_send(i, _):
-            d = NY // 2 + (1 - 2 * lax.rem(i, 2)) * ((i + 1) // 2)
+        def add_and_send(i):
+            d = around(i, NY)
             block = lax.rem(y + d, NY)
             codes_y[h, block], peaks_y[h, block] = coded(add_x(block))
             for copy in y_copies(h, d, block):
                 copy.start()
-            return 0
-
-        lax.fori_loop(0, NY - 1, add_and_send, 0)
+
+        each(NY - 1, add_and_send)
         sums[h] = add_x(y)
 
     sum_x(0)
 
-    for d in (2, 1, 3):
-        for copy in x_copies(1, d):
-            copy.wait_send()
-    for d in range(1, NY):
-        w_y(d, lax.rem(y + NY - d, NY)).wait_recv()
+    each(NX - 1, lambda i: wait_sent_x(i, 1))
+    each(NY - 1, lambda i: w_y(i + 1, lax.rem(y + NY - 1 - i, NY)).wait_recv())
 
     def w_x(d, column):
         to = device(lax.rem(x + d, NX), y, z, core)
         return remote(own_w.at[:, column], own_w.at[:, column], send_wx.at[d - 1], recv_wx.at[d - 1], to)
 
-    for d in (2, 1, 3):
-        w_x(d, x).start()
+    each(NX - 1, lambda i: w_x(around(i, NX), x).start())
 
     scale = F32(1.0 / math.sqrt(NX * NY * NZ * 2 * TOK))
     reducing = low < REDUCERS
@@ -298,30 +301,32 @@
         return remote(rows, rows, send_g.at[d - 1], recv_g.at[row], to)
 
     def send_sums(h):
-        for d in range(1, NY):
-            for copy in y_copies(h, d, y):
+        def wait_y(i):
+            for copy in y_copies(h, i + 1, y):
                 copy.wait_recv()
+
+        each(NY - 1, wait_y)
         value = sums[h]
         for d in range(1, NY):
             value = value + decoded(codes_y_in[h, d - 1], peaks_y_in[h, d - 1])
         total[h] = value.reshape(REDUCERS, 8, KVW)
-        for j in range(REDUCERS):
-
+
+        def send(j):
             @pl.when(z != h * HALF + j)
-            def _(j=j):
+            def _():
                 z_copy(h, j, z).start()
+
+        each(REDUCERS, send)
 
     def reduce_sums(h):
         @pl.when(jnp.logical_and(half == h, reducing))
         def _():
-            for d in range(1, NZ):
-                z_copy(h, 0, lax.rem(z + d, NZ)).wait_recv()
+            each(NZ - 1, lambda i: z_copy(h, 0, lax.rem(z + i + 1, NZ)).wait_recv())
             value = total[h, low]
             for d in range(1, NZ):
                 value = value + total_in[lax.rem(z + d, NZ)]
             final[core, rows_of(low), :] = value * scale
-            for d in (3, 2, 4, 1, 5):
-                g_copy(low, d).start()
+            each(HALF - 1, lambda i: g_copy(low, around(i, HALF)).start())
 
     @pl.when(jnp.logical_not(edge))
     def _():
@@ -332,23 +337,32 @@
     send_sums(1)
     reduce_sums(0)
 
-    for d in range(1, NX):
-        w_x(d, lax.rem(x + NX - d, NX)).wait_recv()
+    each(NX - 1, lambda i: w_x(i + 1, lax.rem(x + NX - 1 - i, NX)).wait_recv())
     w_c = remote(own_w, other_w, send_c.at[3], recv_c.at[3], sibling)
     w_c.start()
 
-    def products(weights, which, columns, store):
-        grad = over_cols(cot[0], weights[:, 0:KVW]) + over_cols(cot[1], weights[:, KVW:COLS])
-        tgrad[which] = grad.astype(BF16)
-        out = pltpu.make_async_copy(tgrad.at[which], tokens_grad.at[:, pl.ds(columns, DH)], store_sem.at[store])
+    def products(weights, which, first):
+        def tile(t):
+            rows = weights[pl.ds(t * 2, 2)].reshape(256, COLS)
+            at = pl.ds(pl.multiple_of(t * 256, 256), 256)
+            grad = over_cols(cot[0], rows[:, 0:KVW]) + over_cols(cot[1], rows[:, KVW:COLS])
+            tgrad[which, :, at] = grad.astype(BF16)
+            left = tok[:, pl.ds(pl.multiple_of(which * DH + t * 256, 256), 256)]
+            kv[...] = kv[...] + jnp.dot(left, rows, preferred_element_type=F32)
+
+        if first:
+            kv[...] = jnp.zeros_like(kv)
+        each(NY // 2, tile)
+        columns = pl.ds(pl.multiple_of(which * DH, DH), DH)
+        out = pltpu.make_async_copy(tgrad.at[which], tokens_grad.at[:, columns], store_sem.at[0 if first else 1])
         out.start()
-        return out, jnp.dot(tok[:, pl.ds(columns, DH)], weights, preferred_element_type=F32)
-
-    out_mine, kv[...] = products(own_w[...].reshape(DH, COLS), core, mine, 0)
+        return out
+
+    out_mine = products(own_w, core, True)
     reduce_sums(1)
     w_c.wait_recv()
-    out_theirs, rest = products(other_w[...].reshape(DH, COLS), 1 - core, theirs, 1)
-    kv_out[...] = (kv[...] + rest).astype(BF16)
+    out_theirs = products(other_w, 1 - core, False)
+    kv_out[...] = kv[...].astype(BF16)
     outs = [
         pltpu.make_async_copy(kv_out.at[:, pl.ds(0, KVW)], keys, store_sem.at[2]),
         pltpu.make_async_copy(kv_out.at[:, pl.ds(KVW, KVW)], values, store_sem.at[3]),
@@ -356,11 +370,12 @@
     for out in outs:
         out.start()
 
-    for j in range(REDUCERS):
-
+    def wait_rows(j):
         @pl.when(low != j)
-        def _(j=j):
+        def _():
             g_copy(j, 1).wait_recv()
+
+    each(REDUCERS, wait_rows)
 
     final_c = remote(final.at[core], final.at[core], send_c.at[4], recv_c.at[4], sibling)
     final_c.start()
@@ -378,29 +393,29 @@
 
     @pl.when(jnp.logical_and(home, edge))
     def _():
-        for k in (1, 2, 3):
-            w_z(k).wait_send()
-
-    for h in range(2):
-        for d in range(1, NY):
-            for copy in y_copies(h, d, y):
+        each(HALF // 2, lambda i: w_z(i + 1).wait_send())
+
+    def sent_y(i):
+        for h in range(2):
+            for copy in y_copies(h, i + 1, y):
                 copy.wait_send()
-        for j in range(REDUCERS):
+        w_y(i + 1, y).wait_send()
+
+    def sent_z(j):
+        for h in range(2):
 
             @pl.when(z != h * HALF + j)
-            def _(h=h, j=j):
+            def _(h=h):
                 z_copy(h, j, z).wait_send()
 
-    for d in range(1, NY):
-        w_y(d, y).wait_send()
-    for d in range(1, NX):
-        w_x(d, x).wait_send()
+    each(NY - 1, sent_y)
+    each(REDUCERS, sent_z)
+    each(NX - 1, lambda i: w_x(i + 1, x).wait_send())
     w_c.wait_send()
 
     @pl.when(reducing)
     def _():
-        for d in range(1, HALF):
-            g_copy(low, d).wait_send()
+        each(HALF - 1, lambda i: g_copy(low, i + 1).wait_send())
 
     final_c.wait_send()
     out_mine.wait()

time: 54 us -> 54 us (level)
  no operation moved by 1% of the time
where the time goes in v5:
time: 54 us; the launch traced here: 53.9 us
  Pallas kernels  53.2 us (99%)
  between operations  0.64 us (1%)
    pallas_call x1, Pallas kernels, on_device(): pl.pallas_call(kernel, out_shape=results, in_specs=[anywhere] * 7, out_sp...  51.1 us
    pallas_call x1, Pallas kernels, on_device(): pl.pallas_call(place, out_shape=results, in_specs=[anywhere] * 5, out_spe...  2.15 us

profile of v5, /device:TPU:1, one launch (start us, length us, event | category | flops | bytes accessed | tf_op | source)
XLA Modules:
  0.0 53.9 jit_solution(18054818191480998943)
XLA Ops:
  0.6 51.1 %projections.1 = (bf16[256,256]{1,0:T(8,128)(2,1)}, bf16[256,256]{1,0:T(8,128)(2,1)}, bf16[256,2048]{1,0:T(8,128)(2,1)}, f32[32,256]{1,0:T(8,128)}, f32[32,256]{1,0:T(8,128)}) custom-call(bf16[256,2048]{1,0:T(8,128)(2,1)} %tokens.1, bf16[256,256]{1,0:T(8,128)(2,1)} %key_cot.1, bf16[256,256]{1,0:T(8,128)(2,1)} %value_cot.1, bf16[32,256]{1,0:T(8,128)(2,1)} %key_mant.1, ...), custom_call_target="tpu_custom_call" | custom-call | tf_op jit(solution)/shard_map/projections/pallas_call | solution.py:459
  51.7 2.1 %place.1 = (bf16[256,256]{1,0:T(8,128)(2,1)}, bf16[256,256]{1,0:T(8,128)(2,1)}, bf16[256,2048]{1,0:T(8,128)(2,1)}, f32[32,256]{1,0:T(8,128)}, f32[32,256]{1,0:T(8,128)}) custom-call(bf16[256,256]{1,0:T(8,128)(2,1)} %get-tuple-element.10.refs_0_, bf16[256,256]{1,0:T(8,128)(2,1)} %get-tuple-element.11.refs_1_, bf16[256,2048]{1,0:T(8,128)(2,1)} %get-tuple-element.12.refs_2_, ...), custom_call_target="tpu_custom_call" | custom-call | tf_op jit(solution)/shard_map/place/pallas_call | solution.py:506

commit v6 on v5

--- a/solution.py
+++ b/solution.py
@@ -335,11 +335,11 @@
     send_sums(0)
     sum_x(1)
     send_sums(1)
-    reduce_sums(0)
 
     each(NX - 1, lambda i: w_x(i + 1, lax.rem(x + NX - 1 - i, NX)).wait_recv())
     w_c = remote(own_w, other_w, send_c.at[3], recv_c.at[3], sibling)
     w_c.start()
+    reduce_sums(0)
 
     def products(weights, which, first):
         def tile(t):

time: 54 us -> 54 us (level)
  no operation moved by 1% of the time
where the time goes in v6:
time: 54 us; the launch traced here: 53.9 us
  Pallas kernels  53.2 us (99%)
  between operations  0.64 us (1%)
    pallas_call x1, Pallas kernels, on_device(): pl.pallas_call(kernel, out_shape=results, in_specs=[anywhere] * 7, out_sp...  51.1 us
    pallas_call x1, Pallas kernels, on_device(): pl.pallas_call(place, out_shape=results, in_specs=[anywhere] * 5, out_spe...  2.15 us

profile of v6, /device:TPU:1, one launch (start us, length us, event | category | flops | bytes accessed | tf_op | source)
XLA Modules:
  0.0 53.9 jit_solution(3815413705649007439)
XLA Ops:
  0.6 51.1 %projections.1 = (bf16[256,256]{1,0:T(8,128)(2,1)}, bf16[256,256]{1,0:T(8,128)(2,1)}, bf16[256,2048]{1,0:T(8,128)(2,1)}, f32[32,256]{1,0:T(8,128)}, f32[32,256]{1,0:T(8,128)}) custom-call(bf16[256,2048]{1,0:T(8,128)(2,1)} %tokens.1, bf16[256,256]{1,0:T(8,128)(2,1)} %key_cot.1, bf16[256,256]{1,0:T(8,128)(2,1)} %value_cot.1, bf16[32,256]{1,0:T(8,128)(2,1)} %key_mant.1, ...), custom_call_target="tpu_custom_call" | custom-call | tf_op jit(solution)/shard_map/projections/pallas_call | solution.py:459
  51.7 2.1 %place.1 = (bf16[256,256]{1,0:T(8,128)(2,1)}, bf16[256,256]{1,0:T(8,128)(2,1)}, bf16[256,2048]{1,0:T(8,128)(2,1)}, f32[32,256]{1,0:T(8,128)}, f32[32,256]{1,0:T(8,128)}) custom-call(bf16[256,256]{1,0:T(8,128)(2,1)} %get-tuple-element.10.refs_0_, bf16[256,256]{1,0:T(8,128)(2,1)} %get-tuple-element.11.refs_1_, bf16[256,2048]{1,0:T(8,128)(2,1)} %get-tuple-element.12.refs_2_, ...), custom_call_target="tpu_custom_call" | custom-call | tf_op jit(solution)/shard_map/place/pallas_call | solution.py:506
